TPU v7x, 512 devices: a whole 4x4x16 slice. The times are simulated.
512 devices in a mesh: blk: 128 (over y, x, z_lo), rep: 4 (over z_hi, core).
Axes of the slice: x: 4, y: 4, z: 16 (z_hi: 2, z_lo: 8; z = z_hi * 8 + z_lo), core: 2. Of those that a mesh axis runs over, the one named last changes fastest.
Arguments:
- jacobian: float32 [32768, 4096], P(('blk', 'rep')), may hold values from -0.09375 to 0.09375
- cell_weight: float32 [4096], replicated, may hold values from 0.4 to 2
- neighbors: int32 [6, 4096], replicated, may hold values from -1 to 4095, as said below
Outputs:
- band: float32 [7, 32768, 256], P(None, 'blk', 'rep')
Inputs may be any that keep to these rules, and one draw needn't show every extreme that they name: neighbors lists the face neighbours of the cells of a 32 x 32 x 4 grid under a numbering of the cells; the relation is symmetric.
All inputs are finite; a program needn't handle non-finite values.
Results may differ from a plain program's by a relative error of at most 0.0001.
Values sent between devices are 32-bit elements; how exact they have to be, the bound alone decides.
A program may use at most 64 MiB of HBM per device.

v0:
```python
import jax
import jax.numpy as jnp
from jax import lax
from jax.sharding import PartitionSpec as P

HALF = 3


def shifted(block, axis, distance):
    devices = range(lax.axis_size(axis))
    route = [((i - distance) % len(devices), i) for i in devices]
    return lax.ppermute(block, axis, route)


def per_device(jacobian, cell_weight, neighbors):
    scaled = jacobian * cell_weight[None, :]
    total = scaled
    for direction in range(6):
        index = neighbors[direction]
        safe = jnp.maximum(index, 0)
        picked = jnp.take(scaled, safe, axis=1)
        present = (index >= 0).astype(jnp.float32)
        total = total + 0.15 * picked * present[None, :]
    smoothed = total * cell_weight[None, :]
    panel = lax.all_gather(smoothed, "rep", axis=0, tiled=True)

    def tile_with(quarter):
        return jnp.einsum("rc,qc->rq", panel, quarter, precision=lax.Precision.HIGHEST)

    tiles = [None] * (2 * HALF + 1)
    tiles[HALF] = tile_with(jacobian)
    ahead = jacobian
    behind = jacobian
    for step in range(1, HALF + 1):
        ahead = shifted(ahead, "blk", -1)
        behind = shifted(behind, "blk", 1)
        tiles[HALF + step] = tile_with(ahead)
        tiles[HALF - step] = tile_with(behind)
    return jnp.stack(tiles, 0)


def solution(mesh):
    return jax.shard_map(
        per_device,
        mesh=mesh,
        in_specs=(P(("blk", "rep"), None), P(), P()),
        out_specs=P(None, "blk", "rep"),
        check_vma=False,
    )
```

profile of v0, /device:TPU:158, one launch (start us, length us, event | category | flops | bytes accessed | tf_op | source)
XLA Modules:
  0.0 390.7 jit_solution(1585450793296040983)
XLA Ops:
  6.5 1.4 slice_maximum_fusion.5
  8.1 1.4 compare_select_fusion.5
  9.5 3.2 copy.5
  12.7 2.2 broadcast_multiply_fusion
  14.9 14.2 %gather_fusion.4 = f32[4096,64]{1,0:T(8,128)} fusion(f32[64,4096]{0,1:T(8,128)S(1)} %broadcast_multiply_fusion, s32[4096]{0:T(1024)S(1)} %get-tuple-element.22), kind=kCustom, calls=%fused_computation.4.clone | custom fusion | bytes 2113536 | tf_op jit(solution)/shard_map/jit(_take)/gather | solution.py:21
  29.1 14.2 %gather_fusion = f32[4096,64]{1,0:T(8,128)} fusion(f32[64,4096]{0,1:T(8,128)S(1)} %broadcast_multiply_fusion, s32[4096]{0:T(1024)S(1)} %get-tuple-element.18), kind=kCustom, calls=%fused_computation.clone | custom fusion | bytes 2113536 | tf_op jit(solution)/shard_map/jit(_take)/gather | solution.py:21
  43.3 14.2 %gather_fusion.1 = f32[4096,64]{1,0:T(8,128)} fusion(f32[64,4096]{0,1:T(8,128)S(1)} %broadcast_multiply_fusion, s32[4096]{0:T(1024)S(1)} %get-tuple-element.19), kind=kCustom, calls=%fused_computation.1.clone | custom fusion | bytes 2113536 | tf_op jit(solution)/shard_map/jit(_take)/gather | solution.py:21
  57.5 14.2 %gather_fusion.2 = f32[4096,64]{1,0:T(8,128)} fusion(f32[64,4096]{0,1:T(8,128)S(1)} %broadcast_multiply_fusion, s32[4096]{0:T(1024)S(1)} %get-tuple-element.20), kind=kCustom, calls=%fused_computation.2.clone | custom fusion | bytes 2113536 | tf_op jit(solution)/shard_map/jit(_take)/gather | solution.py:21
  71.7 14.2 %gather_fusion.3 = f32[4096,64]{1,0:T(8,128)} fusion(f32[64,4096]{0,1:T(8,128)S(1)} %broadcast_multiply_fusion, s32[4096]{0:T(1024)S(1)} %get-tuple-element.21), kind=kCustom, calls=%fused_computation.3.clone | custom fusion | bytes 2113536 | tf_op jit(solution)/shard_map/jit(_take)/gather | solution.py:21
  85.9 14.2 %gather_fusion.5 = f32[4096,64]{1,0:T(8,128)} fusion(f32[64,4096]{0,1:T(8,128)S(1)} %broadcast_multiply_fusion, s32[4096]{0:T(1024)S(1)} %get-tuple-element.23), kind=kCustom, calls=%fused_computation.5.clone | custom fusion | bytes 2113536 | tf_op jit(solution)/shard_map/jit(_take)/gather | solution.py:21
  100.1 12.3 %fusion.1 = f32[64,4096]{0,1:T(8,128)S(1)} fusion(f32[4096,64]{1,0:T(8,128)} %gather_fusion.5, f32[4096,64]{1,0:T(8,128)} %gather_fusion.4, f32[4096,64]{1,0:T(8,128)} %gather_fusion.3, f32[4096,64]{1,0:T(8,128)} %gather_fusion.2, f32[4096,64]{1,0:T(8,128)} %gather_fusion.1, f32[4096,64]{1,0:T(8,128)} %gather_fusion, f32[4096]{0:T(1024)S(1)} %bitcast.107, ...), kind=kLoop, calls=%fused_computation.8 | loop fusion | flops 5242880 | bytes 8527872 | tf_op jit(solution)/shard_map/mul | solution.py:24
  112.4 1.6 copy.6
  114.0 0.0 all-gather.2.cloned.1.call-update
  114.0 3.8 collective-permute-start
  117.8 3.2 collective-permute-start.3
  121.1 110.8 %collective-permute-done = f32[64,4096]{1,0:T(8,128)S(1)} collective-permute-done((f32[64,4096]{1,0:T(8,128)S(1)}, f32[64,4096]{1,0:T(8,128)S(1)}, u32[]{:S(2)}, u32[]{:S(2)}) %collective-permute-start) | collective-permute-done | bytes 1048608 | tf_op jit(solution)/shard_map/ppermute | solution.py:12
  231.9 7.3 %collective-permute-start.1 = (f32[64,4096]{1,0:T(8,128)S(1)}, f32[64,4096]{1,0:T(8,128)S(1)}, u32[]{:S(2)}, u32[]{:S(2)}) collective-permute-start(f32[64,4096]{1,0:T(8,128)S(1)} %collective-permute-done), channel_id=1, source_target_pairs={{508,0},{0,4},{4,8},{8,12},{12,16},{16,20},{20,24},{24,28},{28,32}... | collective-permute-start | bytes 3145736 | tf_op jit(solution)/shard_map/ppermute | solution.py:12
  239.2 20.6 %collective-permute-done.3 = f32[64,4096]{1,0:T(8,128)S(1)} collective-permute-done((f32[64,4096]{1,0:T(8,128)S(1)}, f32[64,4096]{1,0:T(8,128)S(1)}, u32[]{:S(2)}, u32[]{:S(2)}) %collective-permute-start.3) | collective-permute-done | bytes 1048608 | tf_op jit(solution)/shard_map/ppermute | solution.py:12
  259.8 3.9 %collective-permute-start.4 = (f32[64,4096]{1,0:T(8,128)S(1)}, f32[64,4096]{1,0:T(8,128)}, u32[]{:S(2)}, u32[]{:S(2)}) collective-permute-start(f32[64,4096]{1,0:T(8,128)S(1)} %collective-permute-done.3), channel_id=1, source_target_pairs={{4,0},{8,4},{12,8},{16,12},{20,16},{24,20},{28,24},{32,28},{36,32}... | collective-permute-start | bytes 3145736 | tf_op jit(solution)/shard_map/ppermute | solution.py:12
  263.7 37.6 %collective-permute-done.1 = f32[64,4096]{1,0:T(8,128)S(1)} collective-permute-done((f32[64,4096]{1,0:T(8,128)S(1)}, f32[64,4096]{1,0:T(8,128)S(1)}, u32[]{:S(2)}, u32[]{:S(2)}) %collective-permute-start.1) | collective-permute-done | bytes 1048608 | tf_op jit(solution)/shard_map/ppermute | solution.py:12
  301.3 1.9 collective-permute-start.2
  303.2 1.2 collective-permute-done.4
  304.4 4.8 %collective-permute-start.5 = (f32[64,4096]{1,0:T(8,128)}, f32[64,4096]{1,0:T(8,128)}, u32[]{:S(2)}, u32[]{:S(2)}) collective-permute-start(f32[64,4096]{1,0:T(8,128)} %collective-permute-done.4), channel_id=1, source_target_pairs={{4,0},{8,4},{12,8},{16,12},{20,16},{24,20},{28,24},{32,28},{36,32}... | collective-permute-start | bytes 3145736 | tf_op jit(solution)/shard_map/ppermute | solution.py:12
  309.2 40.4 %collective-permute-done.2 = f32[64,4096]{1,0:T(8,128)} collective-permute-done((f32[64,4096]{1,0:T(8,128)S(1)}, f32[64,4096]{1,0:T(8,128)}, u32[]{:S(2)}, u32[]{:S(2)}) %collective-permute-start.2) | collective-permute-done | bytes 1048608 | tf_op jit(solution)/shard_map/ppermute | solution.py:12
  349.6 6.6 %fusion.13 = f32[7,256,64]{1,2,0:T(8,128)S(1)} fusion(f32[256,4096]{1,0:T(8,128)} %all-gather.2.cloned.1.call-done, f32[64,4096]{1,0:T(8,128)} %collective-permute-done.2), kind=kOutput, calls=%fused_computation.32 | convolution fusion | flops 805306368 | bytes 5308416 | tf_op jit(solution)/shard_map/rc,qc->rq/dot_general | solution.py:28
  356.2 3.9 %fusion.12 = f32[7,256,64]{1,2,0:T(8,128)S(1)} fusion(f32[7,256,64]{1,2,0:T(8,128)S(1)} %fusion.13, f32[256,4096]{1,0:T(8,128)S(1)} %copy-done, f32[64,4096]{1,0:T(8,128)S(1)} %copy-done.3), kind=kOutput, calls=%fused_computation.30 | convolution fusion | flops 805306368 | bytes 5308416 | tf_op jit(solution)/shard_map/rc,qc->rq/dot_general | solution.py:28
  360.1 3.9 %fusion.11 = f32[7,256,64]{1,2,0:T(8,128)S(1)} fusion(f32[7,256,64]{1,2,0:T(8,128)S(1)} %fusion.12, f32[256,4096]{1,0:T(8,128)S(1)} %copy-done, f32[64,4096]{1,0:T(8,128)S(1)} %collective-permute-done), kind=kOutput, calls=%fused_computation.28 | convolution fusion | flops 805306368 | bytes 5308416 | tf_op jit(solution)/shard_map/rc,qc->rq/dot_general | solution.py:28
  364.1 3.9 %fusion.10 = f32[7,256,64]{1,2,0:T(8,128)S(1)} fusion(f32[7,256,64]{1,2,0:T(8,128)S(1)} %fusion.11, f32[256,4096]{1,0:T(8,128)S(1)} %copy-done, f32[64,4096]{1,0:T(8,128)S(1)} %copy-done.1), kind=kOutput, calls=%fused_computation.26 | convolution fusion | flops 805306368 | bytes 5308416 | tf_op jit(solution)/shard_map/rc,qc->rq/dot_general | solution.py:28
  368.0 4.2 %fusion.9 = f32[7,256,64]{1,2,0:T(8,128)S(1)} fusion(f32[7,256,64]{1,2,0:T(8,128)S(1)} %fusion.10, f32[256,4096]{1,0:T(8,128)S(1)} %copy-done, f32[64,4096]{1,0:T(8,128)S(1)} %collective-permute-done.3), kind=kOutput, calls=%fused_computation.24 | convolution fusion | flops 805306368 | bytes 5308416 | tf_op jit(solution)/shard_map/rc,qc->rq/dot_general | solution.py:28
  372.2 5.2 %fusion.8 = f32[7,256,64]{1,2,0:T(8,128)S(1)} fusion(f32[7,256,64]{1,2,0:T(8,128)S(1)} %fusion.9, f32[256,4096]{1,0:T(8,128)S(1)} %copy-done, f32[64,4096]{1,0:T(8,128)} %collective-permute-done.4), kind=kOutput, calls=%fused_computation.22 | convolution fusion | flops 805306368 | bytes 5308416 | tf_op jit(solution)/shard_map/rc,qc->rq/dot_general | solution.py:28
  377.4 0.8 copy-done.5
  378.1 5.8 %fusion.7 = f32[7,256,64]{1,2,0:T(8,128)} fusion(f32[7,256,64]{1,2,0:T(8,128)} %copy-done.5, f32[256,4096]{1,0:T(8,128)S(1)} %copy-done, f32[64,4096]{1,0:T(8,128)} %collective-permute-done.5), kind=kOutput, calls=%fused_computation.20 | convolution fusion | flops 805306368 | bytes 5308416 | tf_op jit(solution)/shard_map/rc,qc->rq/dot_general | solution.py:28
  (20 shorter events, 0.1 us)
Async XLA Ops:
  6.5 6.2 %copy-start.4 = (f32[4096]{0:T(1024)S(1)}, f32[4096]{0:T(1024)}, u32[]{:S(2)}) copy-start(f32[4096]{0:T(1024)} %param.6) | copy-start | bytes 49156
  6.5 343.1 %all-gather.2.cloned.1.call-start = ((), (), s32[]{:S(2)}) async-start(), calls=%async_computation | async-start | bytes 5242880 | tf_op jit(solution)/shard_map/all_gather | solution.py:25
  112.4 1.6 copy-start.1
  114.0 117.9 %collective-permute-start = (f32[64,4096]{1,0:T(8,128)S(1)}, f32[64,4096]{1,0:T(8,128)S(1)}, u32[]{:S(2)}, u32[]{:S(2)}) collective-permute-start(f32[64,4096]{1,0:T(8,128)S(1)} %copy-done.1), channel_id=1, source_target_pairs={{508,0},{0,4},{4,8},{8,12},{12,16},{16,20},{20,24},{24,28},{28,32}... | collective-permute-start | bytes 3145736 | tf_op jit(solution)/shard_map/ppermute | solution.py:12
  117.8 141.9 %collective-permute-start.3 = (f32[64,4096]{1,0:T(8,128)S(1)}, f32[64,4096]{1,0:T(8,128)S(1)}, u32[]{:S(2)}, u32[]{:S(2)}) collective-permute-start(f32[64,4096]{1,0:T(8,128)S(1)} %copy-done.1), channel_id=1, source_target_pairs={{4,0},{8,4},{12,8},{16,12},{20,16},{24,20},{28,24},{32,28},{36,32}... | collective-permute-start | bytes 3145736 | tf_op jit(solution)/shard_map/ppermute | solution.py:12
  231.9 69.4 %collective-permute-start.1 = (f32[64,4096]{1,0:T(8,128)S(1)}, f32[64,4096]{1,0:T(8,128)S(1)}, u32[]{:S(2)}, u32[]{:S(2)}) collective-permute-start(f32[64,4096]{1,0:T(8,128)S(1)} %collective-permute-done), channel_id=1, source_target_pairs={{508,0},{0,4},{4,8},{8,12},{12,16},{16,20},{20,24},{24,28},{28,32}... | collective-permute-start | bytes 3145736 | tf_op jit(solution)/shard_map/ppermute | solution.py:12
  259.8 44.6 %collective-permute-start.4 = (f32[64,4096]{1,0:T(8,128)S(1)}, f32[64,4096]{1,0:T(8,128)}, u32[]{:S(2)}, u32[]{:S(2)}) collective-permute-start(f32[64,4096]{1,0:T(8,128)S(1)} %collective-permute-done.3), channel_id=1, source_target_pairs={{4,0},{8,4},{12,8},{16,12},{20,16},{24,20},{28,24},{32,28},{36,32}... | collective-permute-start | bytes 3145736 | tf_op jit(solution)/shard_map/ppermute | solution.py:12
  301.3 3.1 copy-start.2
  301.3 48.3 %collective-permute-start.2 = (f32[64,4096]{1,0:T(8,128)S(1)}, f32[64,4096]{1,0:T(8,128)}, u32[]{:S(2)}, u32[]{:S(2)}) collective-permute-start(f32[64,4096]{1,0:T(8,128)S(1)} %collective-permute-done.1), channel_id=1, source_target_pairs={{508,0},{0,4},{4,8},{8,12},{12,16},{16,20},{20,24},{24,28},{28,32}... | collective-permute-start | bytes 3145736 | tf_op jit(solution)/shard_map/ppermute | solution.py:12
  304.4 72.9 %collective-permute-start.5 = (f32[64,4096]{1,0:T(8,128)}, f32[64,4096]{1,0:T(8,128)}, u32[]{:S(2)}, u32[]{:S(2)}) collective-permute-start(f32[64,4096]{1,0:T(8,128)} %collective-permute-done.4), channel_id=1, source_target_pairs={{4,0},{8,4},{12,8},{16,12},{20,16},{24,20},{28,24},{32,28},{36,32}... | collective-permute-start | bytes 3145736 | tf_op jit(solution)/shard_map/ppermute | solution.py:12
  349.6 6.6 %copy-start = (f32[256,4096]{1,0:T(8,128)S(1)}, f32[256,4096]{1,0:T(8,128)}, u32[]{:S(2)}) copy-start(f32[256,4096]{1,0:T(8,128)} %all-gather.2.cloned.1.call-done) | copy-start | bytes 12582916
  349.6 6.6 %copy-start.3 = (f32[64,4096]{1,0:T(8,128)S(1)}, f32[64,4096]{1,0:T(8,128)}, u32[]{:S(2)}) copy-start(f32[64,4096]{1,0:T(8,128)} %copy-done.2) | copy-start | bytes 3145732
  377.3 0.8 copy-start.5
Sparse Core Ops, SparseCore 0:
  114.1 158.9 all-gather.1
where the time goes:
time: 391 us
  waiting for transfers between devices  211 us (54%)
  local copies, waits for them, and re-layouts  90.7 us (23%)
  matrix products  33.5 us (9%)
  starting transfers between devices  25 us (6%)
  other arithmetic  17.4 us (4%)
  between operations  13.6 us (3%)
    ppermute x6, waiting for transfers between devices, shifted(): return lax.ppermute(block, axis, route)  211 us
    gather x6, local copies, waits for them, and re-layouts, per_device(): picked = jnp.take(scaled, safe, axis=1)  85.2 us
    dot_general x7, matrix products, tile_with(): jnp.einsum('rc,qc->rq', panel, quarter, precision=lax.Precision.HIGHEST)  33.5 us
    ppermute x6, starting transfers between devices, shifted(): return lax.ppermute(block, axis, route)  25 us
    mul x1, other arithmetic, per_device(): smoothed = total * cell_weight[None, :]  12.3 us
  transfers between devices with their start and end apart: 7, of which 5 were waited for; matrix products, arithmetic and copies ran while one was open for 7% of the time, Pallas kernels for 0%

commit v1 on v0

v1 whole, which is shorter than its diff:
```python
import math

import jax
import jax.numpy as jnp
import numpy as np
from jax import lax
from jax.experimental import pallas as pl
from jax.experimental.pallas import tpu as pltpu
from jax.sharding import PartitionSpec as P

F32, BF16 = jnp.float32, jnp.bfloat16
MESH = pl.DeviceIdType.MESH
SIDE = 32
NT = (((1,), (1,)), ((), ()))


def sine(y, n):
    return math.sqrt(2 / 33) * math.sin(math.pi * (y + 1) * (n + 1) / 33)


def lookup(table_ref, index):
    parts = []
    for g in range(4):
        idx = index[8 * g : 8 * g + 8]
        row, lane = idx >> 7, idx & 127
        out = jnp.zeros((8, 128), jnp.int32)
        for s in range(32):
            line = jnp.broadcast_to(table_ref[s : s + 1, :], (8, 128))
            got = jnp.take_along_axis(line, lane, axis=1, mode="promise_in_bounds")
            out = jnp.where(row == s, got, out)
        parts.append(out)
    return jnp.concatenate(parts, 0)


def steps_to_end(near, rounds, table_ref, own):
    value = jnp.where(near >= 0, near + 4096, own)
    for _ in range(rounds):
        table_ref[...] = value
        index = value & 4095
        value = (value - index) + lookup(table_ref, index)
    return value >> 12


def local_kernel(j_ref, w_ref, nb_ref, y_ref, table, first, second, hi, lo, onehot, acc):
    own = lax.broadcasted_iota(jnp.int32, (32, 128), 0) * 128 + lax.broadcasted_iota(jnp.int32, (32, 128), 1)
    missing = [jnp.where(nb_ref[d] < 0, 1.0, 0.0).astype(F32) for d in range(6)]
    count = [jnp.sum(m) for m in missing]

    def pick(flags, arrays):
        total = flags[0] * arrays[0]
        for flag, array in zip(flags[1:], arrays[1:]):
            total = total + flag * array
        return total

    def leading(conds):
        seen, flags = jnp.int32(0), []
        for cond in conds:
            flag = jnp.where(cond, 1, 0) * (1 - seen)
            seen = seen + flag
            flags.append(flag)
        return flags

    nbs = [nb_ref[d] for d in range(6)]
    deep = leading([c > 512.0 for c in count])
    one = leading([c < 512.0 for c in count])
    face = pick([f.astype(F32) for f in one], missing)
    meet = [jnp.sum(face * m) for m in missing]
    two = leading([(c < 512.0) & (m > 0.5) & (f == 0) for c, m, f in zip(count, meet, one)])
    ycoord = steps_to_end(pick(one, nbs), 5, table, own)
    xcoord = steps_to_end(pick(two, nbs), 5, table, own)
    layer = steps_to_end(pick(deep, nbs), 2, table, own)
    first[...] = ycoord >> 2
    second[...] = (ycoord & 3) * 128 + layer * 32 + xcoord

    for s in range(32):
        cols = slice(128 * s, 128 * s + 128)
        js = j_ref[:, cols] * w_ref[s : s + 1, :]
        top = js.astype(BF16)
        rest = (js - top.astype(F32)).astype(BF16)
        arow = jnp.broadcast_to(first[s : s + 1, :], (64, 128))
        for a in range(8):
            mask = jnp.where(arow == a, 1.0, 0.0).astype(BF16)
            hi[64 * a : 64 * a + 64, cols] = top * mask
            lo[64 * a : 64 * a + 64, cols] = rest * mask
        brow = jnp.broadcast_to(second[s : s + 1, :], (512, 128))
        onehot[:, cols] = jnp.where(brow == lax.broadcasted_iota(jnp.int32, (512, 128), 0), 1.0, 0.0).astype(BF16)

    for n in range(2):
        part = slice(256 * n, 256 * n + 256)
        acc[:, part] = lax.dot_general(hi[...], onehot[part, :], NT, preferred_element_type=F32) + lax.dot_general(
            lo[...], onehot[part, :], NT, preferred_element_type=F32
        )

    @pl.loop(0, 8)
    def _(g):
        rows = lambda a: pl.ds(pl.multiple_of(a * 64 + g * 8, 8), 8)
        z = lambda y: acc[rows(y // 4), 128 * (y % 4) : 128 * (y % 4) + 128]
        even, odd = [], []
        for y in range(16):
            p, q = z(y), z(31 - y)
            even.append(p + q)
            odd.append(p - q)
        for n in range(32):
            terms = odd if n % 2 else even
            total = terms[0] * sine(0, n)
            for y in range(1, 16):
                total = total + terms[y] * sine(y, n)
            y_ref[n // 2, pl.ds(pl.multiple_of(g * 8, 8), 8), 128 * (n % 2) : 128 * (n % 2) + 128] = total


def local_part(jacobian, cell_weight, neighbors):
    vmem = pl.BlockSpec(memory_space=pltpu.VMEM)
    return pl.pallas_call(
        local_kernel,
        out_shape=jax.ShapeDtypeStruct((16, 64, 256), F32),
        in_specs=[vmem] * 3,
        out_specs=vmem,
        scratch_shapes=[
            pltpu.VMEM((32, 128), jnp.int32),
            pltpu.VMEM((32, 128), jnp.int32),
            pltpu.VMEM((32, 128), jnp.int32),
            pltpu.VMEM((512, 4096), BF16),
            pltpu.VMEM((512, 4096), BF16),
            pltpu.VMEM((512, 4096), BF16),
            pltpu.VMEM((512, 512), F32),
        ],
        compiler_params=pltpu.CompilerParams(vmem_limit_bytes=40 * 2**20),
    )(jacobian, cell_weight.reshape(32, 128), neighbors.reshape(6, 32, 128))


def task_place(t, k8, e):
    col = t // 2
    half = (t + col) % 2
    return (half * 8 + k8) * 8 + col % 8, (col // 8) * 2 + e


def unless(cond, fn):
    pl.when(jnp.logical_not(cond))(fn)


def band_kernel(
    y_ref, lam_ref, adj_ref, o_ref,
    ra, rb, xhi, xlo, shi, slo, part, r1, r2, fin,
    sa_s, sa_r, sb_s, sb_r, sf_s, sf_r, s1_s, s1_r, s2_s, s2_r, so_s, so_r,
):
    B, R = lax.axis_index("blk"), lax.axis_index("rep")
    pln, zl, zh, e = B // 8, B % 8, R // 2, R % 2
    z = zh * 8 + zl
    half, k8 = pln // 8, pln % 8
    t = 2 * z + (half + zl) % 2

    def is_me(place):
        return (place[0] == B) & (place[1] == R)

    def send(src, dst, s_sem, r_sem, place):
        def there():
            pltpu.make_async_remote_copy(src, dst, s_sem, r_sem, device_id=place, device_id_type=MESH).start()

        def here():
            pltpu.make_async_copy(src, dst, r_sem).start()

        pl.when(is_me(place))(here)
        unless(is_me(place), there)

    def landed(ref, sem):
        pltpu.make_async_copy(ref, ref, sem).wait()

    def sent(ref, sem, place):
        unless(is_me(place), lambda: pltpu.make_async_copy(ref, ref, sem).wait())

    src_half = (zl // 4 + pln) % 2

    def a_to(k):
        return (src_half * 8 + k // 2) * 8 + zl, zh * 2 + k % 2

    def col_of(i):
        return 2 * i + (half + zl // 4) % 2

    def a_from(s):
        return col_of(s // 2) * 8 + zl, zh * 2 + s % 2

    def b_to(i):
        col = col_of(i)
        return pln * 8 + col % 8, (col // 8) * 2 + e

    def b_from(i):
        return pln * 8 + 4 * (t % 2) + i // 2, (i % 2) * 2 + e

    down = task_place((t + 31) % 32, k8, e)
    up = task_place((t + 1) % 32, k8, e)
    other = (B, zh * 2 + 1 - e)

    def mate(i):
        return (half * 8 + i) * 8 + zl, R

    panel = 4 * t + 2 * e + k8 // 4
    gap = k8 % 4

    def o_to(i):
        return (panel + (i // 4) * gap) % 128, i % 4

    def o_from(m):
        j = jnp.where(m < 3, 3 - m, m - 3)
        b = jnp.where(m < 3, (B - j + 128) % 128, B)
        q = 4 * (b % 4) + j
        return task_place(b // 4, q % 8, q // 8)

    barrier = pltpu.get_barrier_semaphore()

    def greet(place):
        unless(
            is_me(place),
            lambda: pl.semaphore_signal(barrier, inc=1, device_id=place, device_id_type=MESH),
        )

    greet(up)
    greet(other)
    pl.loop(0, 16)(lambda s: greet(a_from(s)))
    pl.loop(0, 8)(lambda s: greet(b_from(s)))
    pl.loop(0, 8)(lambda s: greet(mate(s)))
    pl.loop(0, 7)(lambda s: greet(o_from(s)))
    out_count = jnp.where(gap == 0, 4, 8)
    own_a = jnp.where(src_half == half, 1, 0)
    own_b = jnp.where((z + half + zl // 4) % 2 == 0, 1, 0)
    own_o = jnp.where((panel == B) | ((panel + gap) % 128 == B), 1, 0)
    pl.semaphore_wait(barrier, 2 + 16 + 8 + 7 + out_count - own_a - own_b - own_o)

    @pl.loop(0, 16)
    def _(n):
        k = (n + 2 * pln + 2) % 16
        slot = (pln // 2) * 2 + e
        send(y_ref.at[k], ra.at[slot], sa_s.at[k], sa_r.at[slot], a_to(k))

    @pl.loop(0, 16)
    def _(n):
        s = (n + pln + 2 * (z // 2)) % 16
        landed(ra.at[s], sa_r.at[s])
        slot = (zl % 4) * 4 + zh * 2 + s % 2
        send(ra.at[s], rb.at[slot], sb_s.at[s], sb_r.at[slot], b_to(s // 2))

    def split(p):
        rows = pl.ds(pl.multiple_of(p * 256, 256), 256)
        x = rb[pl.ds(p * 4, 4)].reshape(256, 256)
        top = x.astype(BF16)
        rest = (x - top.astype(F32)).astype(BF16)
        xhi[rows, :] = top
        xlo[rows, :] = rest
        return rows, x, top, rest

    @pl.loop(0, 4)
    def _(p):
        @pl.loop(0, 4)
        def _(i):
            landed(rb.at[p * 4 + i], sb_r.at[p * 4 + i])

        @pl.when(p < 3)
        def _():
            send(rb.at[pl.ds(p * 4, 4)], rb.at[pl.ds(16 + p * 4, 4)], sf_s.at[p], sf_r.at[p], down)

        rows, x, top, rest = split(p)
        beside = jnp.dot(top, adj_ref[...], preferred_element_type=F32)
        beside = beside + jnp.dot(rest, adj_ref[...], preferred_element_type=F32)
        smooth = x * lam_ref[pl.ds(2 * k8 + e, 1), :] + 0.15 * beside
        stop = smooth.astype(BF16)
        shi[rows, :] = stop
        slo[rows, :] = (smooth - stop.astype(F32)).astype(BF16)

    @pl.loop(0, 3)
    def _(p):
        landed(rb.at[pl.ds(16 + p * 4, 4)], sf_r.at[p])
        split(p + 4)

    def tile(q):
        p = pl.ds(pl.multiple_of((q // 4) * 256, 256), 256)
        o = pl.ds(pl.multiple_of((q // 4 + q % 4) * 256, 256), 256)
        total = lax.dot_general(shi[p, :], xlo[o, :], NT, preferred_element_type=F32)
        total = total + lax.dot_general(slo[p, :], xhi[o, :], NT, preferred_element_type=F32)
        return total + lax.dot_general(shi[p, :], xhi[o, :], NT, preferred_element_type=F32)

    @pl.loop(0, 8)
    def _(n):
        i = (k8 + 1 + n) % 8
        q = 8 * (1 - e) + i
        part[q] = tile(q)
        send(part.at[q], r1.at[i], s1_s.at[i], s1_r.at[i], other)

    @pl.loop(0, 8)
    def _(n):
        i = (k8 + 1 + n) % 8
        q = 8 * e + i
        total = tile(q)
        landed(r1.at[i], s1_r.at[i])
        part[q] = total + r1[i]

        @pl.when(n < 7)
        def _():
            send(part.at[q], r2.at[k8], s2_s.at[i], s2_r.at[k8], mate(i))

    r2[k8] = part[8 * e + k8]

    @pl.loop(0, 7)
    def _(n):
        i = (k8 + 7 - n) % 8
        landed(r2.at[i], s2_r.at[i])

    total = r2[0]
    for i in range(1, 8):
        total = total + r2[i]
    fin[pl.ds(0, 4)] = total.T.reshape(4, 64, 256)
    fin[pl.ds(4, 4)] = total.reshape(4, 64, 256)

    @pl.loop(0, out_count)
    def _(i):
        m = jnp.where(i < 4, 3 + gap, 3 - gap)
        send(fin.at[i], o_ref.at[m], so_s.at[i], so_r.at[m], o_to(i))

    pl.loop(0, 7)(lambda m: landed(o_ref.at[m], so_r.at[m]))

    pl.loop(0, 16)(lambda k: sent(y_ref.at[k], sa_s.at[k], a_to(k)))
    pl.loop(0, 16)(lambda s: sent(ra.at[s], sb_s.at[s], b_to(s // 2)))
    pl.loop(0, 3)(lambda p: sent(rb.at[pl.ds(p * 4, 4)], sf_s.at[p], down))
    pl.loop(0, 8)(lambda i: sent(part.at[8 * (1 - e) + i], s1_s.at[i], other))
    pl.loop(0, 8)(lambda i: sent(part.at[8 * e + i], s2_s.at[i], mate(i)))
    pl.loop(0, out_count)(lambda i: sent(fin.at[i], so_s.at[i], o_to(i)))


def band_part(spectral):
    lane = np.arange(128)
    x, layer = lane % 32, lane // 32
    near = np.abs(x[:, None] - x[None, :]) + np.abs(layer[:, None] - layer[None, :]) == 1
    adjacency = jnp.asarray(np.kron(np.eye(2), near), BF16)
    n = np.arange(32)
    lam = 1 + 0.15 * 2 * np.cos(np.pi * (n + 1) / 33)
    lam = jnp.asarray(np.repeat(lam, 128).reshape(16, 256), F32)
    vmem = pl.BlockSpec(memory_space=pltpu.VMEM)
    dma = pltpu.SemaphoreType.DMA
    counts = (16, 16, 16, 16, 3, 3, 8, 8, 8, 8, 8, 7)
    return pl.pallas_call(
        band_kernel,
        out_shape=jax.ShapeDtypeStruct((7, 64, 256), F32),
        in_specs=[vmem] * 3,
        out_specs=vmem,
        scratch_shapes=[
            pltpu.VMEM((16, 64, 256), F32),
            pltpu.VMEM((28, 64, 256), F32),
            pltpu.VMEM((1792, 256), BF16),
            pltpu.VMEM((1792, 256), BF16),
            pltpu.VMEM((1024, 256), BF16),
            pltpu.VMEM((1024, 256), BF16),
            pltpu.VMEM((16, 256, 256), F32),
            pltpu.VMEM((8, 256, 256), F32),
            pltpu.VMEM((8, 256, 256), F32),
            pltpu.VMEM((8, 64, 256), F32),
        ]
        + [dma((c,)) for c in counts],
        compiler_params=pltpu.CompilerParams(collective_id=0, has_side_effects=True, vmem_limit_bytes=40 * 2**20),
    )(spectral, lam, adjacency)


def per_device(jacobian, cell_weight, neighbors):
    spectral = local_part(jacobian, cell_weight, neighbors)
    return jnp.swapaxes(band_part(spectral), 1, 2)


def solution(mesh):
    return jax.shard_map(
        per_device,
        mesh=mesh,
        in_specs=(P(("blk", "rep"), None), P(), P()),
        out_specs=P(None, "blk", "rep"),
        check_vma=False,
    )
```

time: 391 us -> 174 us (0.45)
  the two profiles are of different devices: /device:TPU:158 before, /device:TPU:89 now
where the time goes in v1:
time: 174 us
  Pallas kernels  171 us (98%)
  local copies, waits for them, and re-layouts  2.94 us (2%)
    pallas_call x1, Pallas kernels, band_part(): pl.pallas_call(band_kernel, out_shape=jax.ShapeDtypeStruct((7, 64, 256),...  161 us
    pallas_call x1, Pallas kernels, local_part(): pl.pallas_call(local_kernel, out_shape=jax.ShapeDtypeStruct((16, 64, 256)...  9.7 us

profile of v1, /device:TPU:89, one launch (start us, length us, event | category | flops | bytes accessed | tf_op | source)
XLA Modules:
  0.0 173.7 jit_solution(7570130180008794223)
XLA Ops:
  0.0 0.0 copy-start.2
  0.0 0.9 copy.8
  0.9 0.0 copy-done.2
  1.0 0.0 copy-start
  1.0 1.2 copy-done
  2.2 0.0 copy-start.1
  2.2 0.0 copy-start.3
  2.2 9.7 %shard_map.55.y_ref = f32[16,64,256]{2,1,0:T(8,128)S(1)} custom-call(f32[64,4096]{1,0:T(8,128)S(1)} %copy-done, f32[32,128]{1,0:T(8,128)S(1)} %bitcast.8, s32[6,32,128]{2,1,0:T(8,128)S(1)} %bitcast.7), custom_call_target="tpu_custom_call" | custom-call | tf_op jit(solution)/shard_map/pallas_call | solution.py:113
  11.9 0.0 copy-done.1
  11.9 0.0 copy-done.3
  11.9 161.0 %shard_map.56 = f32[7,64,256]{2,1,0:T(8,128)S(1)} custom-call(f32[16,64,256]{2,1,0:T(8,128)S(1)} %shard_map.55.y_ref, f32[16,256]{1,0:T(8,128)S(1)} %copy-done.3, bf16[256,256]{1,0:T(8,128)(2,1)S(1)} %copy-done.1), custom_call_target="tpu_custom_call" | custom-call | tf_op jit(solution)/shard_map/pallas_call | solution.py:338
  172.9 0.8 copy.10
Async XLA Ops:
  0.0 0.9 copy-start.2
  1.0 1.2 copy-start
  2.2 9.7 %copy-start.1 = (bf16[256,256]{1,0:T(8,128)(2,1)S(1)}, bf16[256,256]{1,0:T(8,128)(2,1)}, u32[]{:S(2)}) copy-start(bf16[256,256]{1,0:T(8,128)(2,1)} %constant.4.clone.adj_ref) | copy-start | bytes 393220
  2.2 9.7 %copy-start.3 = (f32[16,256]{1,0:T(8,128)S(1)}, f32[16,256]{1,0:T(8,128)}, u32[]{:S(2)}) copy-start(f32[16,256]{1,0:T(8,128)} %constant.5.clone.lam_ref) | copy-start | bytes 49156

commit v2 on v1

--- a/solution.py
+++ b/solution.py
@@ -129,9 +129,8 @@
 
 
 def task_place(t, k8, e):
-    col = t // 2
-    half = (t + col) % 2
-    return (half * 8 + k8) * 8 + col % 8, (col // 8) * 2 + e
+    z = t % 16
+    return ((t // 16) * 8 + k8) * 8 + z % 8, (z // 8) * 2 + e
 
 
 def unless(cond, fn):
@@ -140,14 +139,14 @@
 
 def band_kernel(
     y_ref, lam_ref, adj_ref, o_ref,
-    ra, rb, xhi, xlo, shi, slo, part, r1, r2, fin,
-    sa_s, sa_r, sb_s, sb_r, sf_s, sf_r, s1_s, s1_r, s2_s, s2_r, so_s, so_r,
+    ra, rb, xhi, xlo, shi, slo, part, r1, r2, across, along,
+    sa_s, sa_r, sb_s, sb_r, sf_s, sf_r, s1_s, s1_r, s2_s, s2_r, sx_s, sy_s, so_r,
 ):
     B, R = lax.axis_index("blk"), lax.axis_index("rep")
     pln, zl, zh, e = B // 8, B % 8, R // 2, R % 2
     z = zh * 8 + zl
     half, k8 = pln // 8, pln % 8
-    t = 2 * z + (half + zl) % 2
+    t = half * 16 + z
 
     def is_me(place):
         return (place[0] == B) & (place[1] == R)
@@ -168,23 +167,15 @@
     def sent(ref, sem, place):
         unless(is_me(place), lambda: pltpu.make_async_copy(ref, ref, sem).wait())
 
-    src_half = (zl // 4 + pln) % 2
-
     def a_to(k):
-        return (src_half * 8 + k // 2) * 8 + zl, zh * 2 + k % 2
-
-    def col_of(i):
-        return 2 * i + (half + zl // 4) % 2
-
-    def a_from(s):
-        return col_of(s // 2) * 8 + zl, zh * 2 + s % 2
+        return (half * 8 + k // 2) * 8 + zl, zh * 2 + k % 2
 
     def b_to(i):
-        col = col_of(i)
-        return pln * 8 + col % 8, (col // 8) * 2 + e
+        there = 2 * i + zl // 4
+        return pln * 8 + there % 8, (there // 8) * 2 + e
 
     def b_from(i):
-        return pln * 8 + 4 * (t % 2) + i // 2, (i % 2) * 2 + e
+        return pln * 8 + 4 * (z % 2) + i // 2, (i % 2) * 2 + e
 
     down = task_place((t + 31) % 32, k8, e)
     up = task_place((t + 1) % 32, k8, e)
@@ -193,17 +184,19 @@
     def mate(i):
         return (half * 8 + i) * 8 + zl, R
 
-    panel = 4 * t + 2 * e + k8 // 4
+    def worked_on(b, j):
+        later = jnp.where((b % 4 == 3) & (j >= 1), 1, 0)
+        q = 4 * (b % 4) + j
+        return task_place((b // 4 + later) % 32, q % 8, q // 8)
+
+    lead = 2 * e + k8 // 4
     gap = k8 % 4
-
-    def o_to(i):
-        return (panel + (i // 4) * gap) % 128, i % 4
+    panel = jnp.where((lead == 3) & (gap >= 1), (4 * t + 127) % 128, 4 * t + lead)
+    facing = (panel + gap) % 128
 
     def o_from(m):
         j = jnp.where(m < 3, 3 - m, m - 3)
-        b = jnp.where(m < 3, (B - j + 128) % 128, B)
-        q = 4 * (b % 4) + j
-        return task_place(b // 4, q % 8, q // 8)
+        return worked_on(jnp.where(m < 3, (B - j + 128) % 128, B), j)
 
     barrier = pltpu.get_barrier_semaphore()
 
@@ -214,50 +207,60 @@
         )
 
     greet(up)
+    greet(down)
     greet(other)
-    pl.loop(0, 16)(lambda s: greet(a_from(s)))
+    pl.loop(0, 16)(lambda s: greet(a_to(s)))
     pl.loop(0, 8)(lambda s: greet(b_from(s)))
     pl.loop(0, 8)(lambda s: greet(mate(s)))
     pl.loop(0, 7)(lambda s: greet(o_from(s)))
+    own_b = jnp.where((z + zl // 4) % 2 == 0, 1, 0)
+    own_o = jnp.where((panel == B) | (facing == B), 1, 0)
     out_count = jnp.where(gap == 0, 4, 8)
-    own_a = jnp.where(src_half == half, 1, 0)
-    own_b = jnp.where((z + half + zl // 4) % 2 == 0, 1, 0)
-    own_o = jnp.where((panel == B) | ((panel + gap) % 128 == B), 1, 0)
-    pl.semaphore_wait(barrier, 2 + 16 + 8 + 7 + out_count - own_a - own_b - own_o)
+    pl.semaphore_wait(barrier, 3 + 15 + 8 + 7 + out_count - own_b - own_o)
 
     @pl.loop(0, 16)
     def _(n):
-        k = (n + 2 * pln + 2) % 16
-        slot = (pln // 2) * 2 + e
-        send(y_ref.at[k], ra.at[slot], sa_s.at[k], sa_r.at[slot], a_to(k))
+        k = 2 * ((k8 + n // 2 + z + 4 * (n % 2)) % 8) + n % 2
+        send(y_ref.at[k], ra.at[2 * k8 + e], sa_s.at[k], sa_r.at[2 * k8 + e], a_to(k))
 
     @pl.loop(0, 16)
     def _(n):
-        s = (n + pln + 2 * (z // 2)) % 16
+        i = (k8 + 32 - z - 4 * e - n // 2) % 8
+        s = 2 * i + n % 2
         landed(ra.at[s], sa_r.at[s])
-        slot = (zl % 4) * 4 + zh * 2 + s % 2
-        send(ra.at[s], rb.at[slot], sb_s.at[s], sb_r.at[slot], b_to(s // 2))
-
-    def split(p):
-        rows = pl.ds(pl.multiple_of(p * 256, 256), 256)
+        slot = (zl % 4) * 4 + zh * 2 + n % 2
+        send(ra.at[s], rb.at[slot], sb_s.at[s], sb_r.at[slot], b_to(i))
+
+    def fwd_slot(n):
+        return jnp.where(n < 4, n, jnp.where(n < 8, n + 8, n - 4))
+
+    @pl.loop(0, 12)
+    def _(n):
+        s = fwd_slot(n)
+        landed(rb.at[s], sb_r.at[s])
+
+        @pl.when(s < 8)
+        def _():
+            send(rb.at[s], rb.at[16 + s], sf_s.at[s], sf_r.at[s], down)
+
+        @pl.when(s >= 12)
+        def _():
+            send(rb.at[s], rb.at[12 + s], sf_s.at[s - 4], sf_r.at[s - 4], up)
+
+    pl.loop(8, 12)(lambda s: landed(rb.at[s], sb_r.at[s]))
+
+    def fetch(p):
         x = rb[pl.ds(p * 4, 4)].reshape(256, 256)
         top = x.astype(BF16)
-        rest = (x - top.astype(F32)).astype(BF16)
+        return x, top, (x - top.astype(F32)).astype(BF16)
+
+    def keep(p, top, rest):
+        rows = pl.ds(pl.multiple_of(p * 256, 256), 256)
         xhi[rows, :] = top
         xlo[rows, :] = rest
-        return rows, x, top, rest
-
-    @pl.loop(0, 4)
-    def _(p):
-        @pl.loop(0, 4)
-        def _(i):
-            landed(rb.at[p * 4 + i], sb_r.at[p * 4 + i])
-
-        @pl.when(p < 3)
-        def _():
-            send(rb.at[pl.ds(p * 4, 4)], rb.at[pl.ds(16 + p * 4, 4)], sf_s.at[p], sf_r.at[p], down)
-
-        rows, x, top, rest = split(p)
+
+    def smoothed(p, x, top, rest):
+        rows = pl.ds(pl.multiple_of(p * 256, 256), 256)
         beside = jnp.dot(top, adj_ref[...], preferred_element_type=F32)
         beside = beside + jnp.dot(rest, adj_ref[...], preferred_element_type=F32)
         smooth = x * lam_ref[pl.ds(2 * k8 + e, 1), :] + 0.15 * beside
@@ -265,28 +268,46 @@
         shi[rows, :] = stop
         slo[rows, :] = (smooth - stop.astype(F32)).astype(BF16)
 
-    @pl.loop(0, 3)
+    @pl.loop(0, 4)
     def _(p):
-        landed(rb.at[pl.ds(16 + p * 4, 4)], sf_r.at[p])
-        split(p + 4)
+        x, top, rest = fetch(p)
+        keep(p, top, rest)
+        smoothed(p, x, top, rest)
+
+    @pl.loop(0, 2)
+    def _(p):
+        pl.loop(0, 4)(lambda s: landed(rb.at[16 + p * 4 + s], sf_r.at[p * 4 + s]))
+        x, top, rest = fetch(4 + p)
+        keep(4 + p, top, rest)
+
+    pl.loop(0, 4)(lambda s: landed(rb.at[24 + s], sf_r.at[8 + s]))
+    smoothed(4, *fetch(6))
 
     def tile(q):
-        p = pl.ds(pl.multiple_of((q // 4) * 256, 256), 256)
-        o = pl.ds(pl.multiple_of((q // 4 + q % 4) * 256, 256), 256)
+        p, j = q // 4, q % 4
+        before = (p == 3) & (j >= 1)
+        p, o = jnp.where(before, 4, p), jnp.where(before, j - 1, p + j)
+        p = pl.ds(pl.multiple_of(p * 256, 256), 256)
+        o = pl.ds(pl.multiple_of(o * 256, 256), 256)
         total = lax.dot_general(shi[p, :], xlo[o, :], NT, preferred_element_type=F32)
         total = total + lax.dot_general(slo[p, :], xhi[o, :], NT, preferred_element_type=F32)
         return total + lax.dot_general(shi[p, :], xhi[o, :], NT, preferred_element_type=F32)
 
+    def turn(n, core):
+        return jnp.where(n < 7, (k8 + 1 + (n + 3 * core + 2 * k8) % 7) % 8, k8)
+
     @pl.loop(0, 8)
     def _(n):
-        i = (k8 + 1 + n) % 8
+        i = turn(n, 1 - e)
         q = 8 * (1 - e) + i
         part[q] = tile(q)
         send(part.at[q], r1.at[i], s1_s.at[i], s1_r.at[i], other)
 
+    upper, lower = pl.ds(0, 128), pl.ds(128, 128)
+
     @pl.loop(0, 8)
     def _(n):
-        i = (k8 + 1 + n) % 8
+        i = turn(n, e)
         q = 8 * e + i
         total = tile(q)
         landed(r1.at[i], s1_r.at[i])
@@ -294,34 +315,59 @@
 
         @pl.when(n < 7)
         def _():
-            send(part.at[q], r2.at[k8], s2_s.at[i], s2_r.at[k8], mate(i))
+            send(part.at[q, upper], r2.at[k8, upper], s2_s.at[i, 0], s2_r.at[k8, 0], mate(i))
+
+    @pl.loop(0, 7)
+    def _(n):
+        i = turn(n, e)
+        send(part.at[8 * e + i, lower], r2.at[k8, lower], s2_s.at[i, 1], s2_r.at[k8, 1], mate(i))
 
     r2[k8] = part[8 * e + k8]
 
-    @pl.loop(0, 7)
-    def _(n):
-        i = (k8 + 7 - n) % 8
-        landed(r2.at[i], s2_r.at[i])
-
-    total = r2[0]
-    for i in range(1, 8):
-        total = total + r2[i]
-    fin[pl.ds(0, 4)] = total.T.reshape(4, 64, 256)
-    fin[pl.ds(4, 4)] = total.reshape(4, 64, 256)
-
-    @pl.loop(0, out_count)
-    def _(i):
-        m = jnp.where(i < 4, 3 + gap, 3 - gap)
-        send(fin.at[i], o_ref.at[m], so_s.at[i], so_r.at[m], o_to(i))
-
-    pl.loop(0, 7)(lambda m: landed(o_ref.at[m], so_r.at[m]))
+    for h, rows in enumerate((upper, lower)):
+
+        @pl.loop(0, 7)
+        def _(n):
+            i = (k8 + 1 + n) % 8
+            landed(r2.at[i, rows], s2_r.at[i, h])
+
+        total = r2[0, rows]
+        for i in range(1, 8):
+            total = total + r2[i, rows]
+        across[h] = total.T.reshape(4, 64, 128)
+        along[h] = total.reshape(2, 64, 256)
+
+        @pl.loop(0, 4)
+        def _(i):
+            r = (i + pln) % 4
+            send(across.at[h, r], o_ref.at[3 + gap, :, rows], sx_s.at[h, r], so_r.at[3 + gap, h], (panel, r))
+
+        @pl.when(gap >= 1)
+        def _():
+            @pl.loop(0, 2)
+            def _(i):
+                send(along.at[h, i], o_ref.at[3 - gap], sy_s.at[h, i], so_r.at[3 - gap, 0], (facing, 2 * h + i))
+
+    pl.loop(0, 3)(lambda m: landed(o_ref.at[m], so_r.at[m, 0]))
+
+    @pl.loop(3, 7)
+    def _(m):
+        landed(o_ref.at[m, :, upper], so_r.at[m, 0])
+        landed(o_ref.at[m, :, lower], so_r.at[m, 1])
 
     pl.loop(0, 16)(lambda k: sent(y_ref.at[k], sa_s.at[k], a_to(k)))
     pl.loop(0, 16)(lambda s: sent(ra.at[s], sb_s.at[s], b_to(s // 2)))
-    pl.loop(0, 3)(lambda p: sent(rb.at[pl.ds(p * 4, 4)], sf_s.at[p], down))
+    pl.loop(0, 8)(lambda s: sent(rb.at[s], sf_s.at[s], down))
+    pl.loop(0, 4)(lambda s: sent(rb.at[12 + s], sf_s.at[8 + s], up))
     pl.loop(0, 8)(lambda i: sent(part.at[8 * (1 - e) + i], s1_s.at[i], other))
-    pl.loop(0, 8)(lambda i: sent(part.at[8 * e + i], s2_s.at[i], mate(i)))
-    pl.loop(0, out_count)(lambda i: sent(fin.at[i], so_s.at[i], o_to(i)))
+
+    for h, rows in enumerate((upper, lower)):
+        pl.loop(0, 8)(lambda i: sent(part.at[8 * e + i, rows], s2_s.at[i, h], mate(i)))
+        pl.loop(0, 4)(lambda r: sent(across.at[h, r], sx_s.at[h, r], (panel, r)))
+
+        @pl.when(gap >= 1)
+        def _():
+            pl.loop(0, 2)(lambda i: sent(along.at[h, i], sy_s.at[h, i], (facing, 2 * h + i)))
 
 
 def band_part(spectral):
@@ -334,7 +380,7 @@
     lam = jnp.asarray(np.repeat(lam, 128).reshape(16, 256), F32)
     vmem = pl.BlockSpec(memory_space=pltpu.VMEM)
     dma = pltpu.SemaphoreType.DMA
-    counts = (16, 16, 16, 16, 3, 3, 8, 8, 8, 8, 8, 7)
+    counts = ((16,),) * 4 + ((12,),) * 2 + ((8,),) * 2 + ((8, 2),) * 2 + ((2, 4), (2, 2), (7, 2))
     return pl.pallas_call(
         band_kernel,
         out_shape=jax.ShapeDtypeStruct((7, 64, 256), F32),
@@ -343,16 +389,17 @@
         scratch_shapes=[
             pltpu.VMEM((16, 64, 256), F32),
             pltpu.VMEM((28, 64, 256), F32),
-            pltpu.VMEM((1792, 256), BF16),
-            pltpu.VMEM((1792, 256), BF16),
-            pltpu.VMEM((1024, 256), BF16),
-            pltpu.VMEM((1024, 256), BF16),
+            pltpu.VMEM((1536, 256), BF16),
+            pltpu.VMEM((1536, 256), BF16),
+            pltpu.VMEM((1280, 256), BF16),
+            pltpu.VMEM((1280, 256), BF16),
             pltpu.VMEM((16, 256, 256), F32),
             pltpu.VMEM((8, 256, 256), F32),
             pltpu.VMEM((8, 256, 256), F32),
-            pltpu.VMEM((8, 64, 256), F32),
+            pltpu.VMEM((2, 4, 64, 128), F32),
+            pltpu.VMEM((2, 2, 64, 256), F32),
         ]
-        + [dma((c,)) for c in counts],
+        + [dma(c) for c in counts],
         compiler_params=pltpu.CompilerParams(collective_id=0, has_side_effects=True, vmem_limit_bytes=40 * 2**20),
     )(spectral, lam, adjacency)
 

time: 174 us -> 147 us (0.84)
  the two profiles are of different devices: /device:TPU:89 before, /device:TPU:1 now
where the time goes in v2:
time: 147 us
  Pallas kernels  144 us (98%)
  local copies, waits for them, and re-layouts  2.94 us (2%)
    pallas_call x1, Pallas kernels, band_part(): pl.pallas_call(band_kernel, out_shape=jax.ShapeDtypeStruct((7, 64, 256),...  134 us
    pallas_call x1, Pallas kernels, local_part(): pl.pallas_call(local_kernel, out_shape=jax.ShapeDtypeStruct((16, 64, 256)...  9.7 us

profile of v2, /device:TPU:1, one launch (start us, length us, event | category | flops | bytes accessed | tf_op | source)
XLA Modules:
  0.0 146.8 jit_solution(3096035670735067312)
XLA Ops:
  0.0 0.0 copy-start.2
  0.0 0.9 copy.8
  0.9 0.0 copy-done.2
  1.0 0.0 copy-start
  1.0 1.2 copy-done
  2.2 0.0 copy-start.1
  2.2 0.0 copy-start.3
  2.2 9.7 %shard_map.55.y_ref = f32[16,64,256]{2,1,0:T(8,128)S(1)} custom-call(f32[64,4096]{1,0:T(8,128)S(1)} %copy-done, f32[32,128]{1,0:T(8,128)S(1)} %bitcast.8, s32[6,32,128]{2,1,0:T(8,128)S(1)} %bitcast.7), custom_call_target="tpu_custom_call" | custom-call | tf_op jit(solution)/shard_map/pallas_call | solution.py:113
  11.9 0.0 copy-done.1
  11.9 0.0 copy-done.3
  11.9 134.1 %shard_map.56 = f32[7,64,256]{2,1,0:T(8,128)S(1)} custom-call(f32[16,64,256]{2,1,0:T(8,128)S(1)} %shard_map.55.y_ref, f32[16,256]{1,0:T(8,128)S(1)} %copy-done.3, bf16[256,256]{1,0:T(8,128)(2,1)S(1)} %copy-done.1), custom_call_target="tpu_custom_call" | custom-call | tf_op jit(solution)/shard_map/pallas_call | solution.py:384
  146.0 0.8 copy.10
Async XLA Ops:
  0.0 0.9 copy-start.2
  1.0 1.2 copy-start
  2.2 9.7 %copy-start.1 = (bf16[256,256]{1,0:T(8,128)(2,1)S(1)}, bf16[256,256]{1,0:T(8,128)(2,1)}, u32[]{:S(2)}) copy-start(bf16[256,256]{1,0:T(8,128)(2,1)} %constant.4.clone.adj_ref) | copy-start | bytes 393220
  2.2 9.7 %copy-start.3 = (f32[16,256]{1,0:T(8,128)S(1)}, f32[16,256]{1,0:T(8,128)}, u32[]{:S(2)}) copy-start(f32[16,256]{1,0:T(8,128)} %constant.5.clone.lam_ref) | copy-start | bytes 49156

commit v3 on v2

--- a/solution.py
+++ b/solution.py
@@ -41,7 +41,7 @@
     return value >> 12
 
 
-def local_kernel(j_ref, w_ref, nb_ref, y_ref, table, first, second, hi, lo, onehot, acc):
+def place_kernel(nb_ref, first, second, table):
     own = lax.broadcasted_iota(jnp.int32, (32, 128), 0) * 128 + lax.broadcasted_iota(jnp.int32, (32, 128), 1)
     missing = [jnp.where(nb_ref[d] < 0, 1.0, 0.0).astype(F32) for d in range(6)]
     count = [jnp.sum(m) for m in missing]
@@ -72,6 +72,8 @@
     first[...] = ycoord >> 2
     second[...] = (ycoord & 3) * 128 + layer * 32 + xcoord
 
+
+def to_grid_order(j_ref, w_ref, first, second, y_ref, hi, lo, onehot, acc):
     for s in range(32):
         cols = slice(128 * s, 128 * s + 128)
         js = j_ref[:, cols] * w_ref[s : s + 1, :]
@@ -108,24 +110,15 @@
             y_ref[n // 2, pl.ds(pl.multiple_of(g * 8, 8), 8), 128 * (n % 2) : 128 * (n % 2) + 128] = total
 
 
-def local_part(jacobian, cell_weight, neighbors):
+def places(neighbors):
     vmem = pl.BlockSpec(memory_space=pltpu.VMEM)
     return pl.pallas_call(
-        local_kernel,
-        out_shape=jax.ShapeDtypeStruct((16, 64, 256), F32),
-        in_specs=[vmem] * 3,
-        out_specs=vmem,
-        scratch_shapes=[
-            pltpu.VMEM((32, 128), jnp.int32),
-            pltpu.VMEM((32, 128), jnp.int32),
-            pltpu.VMEM((32, 128), jnp.int32),
-            pltpu.VMEM((512, 4096), BF16),
-            pltpu.VMEM((512, 4096), BF16),
-            pltpu.VMEM((512, 4096), BF16),
-            pltpu.VMEM((512, 512), F32),
-        ],
-        compiler_params=pltpu.CompilerParams(vmem_limit_bytes=40 * 2**20),
-    )(jacobian, cell_weight.reshape(32, 128), neighbors.reshape(6, 32, 128))
+        place_kernel,
+        out_shape=[jax.ShapeDtypeStruct((32, 128), jnp.int32)] * 2,
+        in_specs=[vmem],
+        out_specs=[vmem] * 2,
+        scratch_shapes=[pltpu.VMEM((32, 128), jnp.int32)],
+    )(neighbors.reshape(6, 32, 128))
 
 
 def task_place(t, k8, e):
@@ -138,7 +131,8 @@
 
 
 def band_kernel(
-    y_ref, lam_ref, adj_ref, o_ref,
+    j_ref, w_ref, first, second, lam_ref, adj_ref, o_ref,
+    y_ref, hi, lo, onehot, acc,
     ra, rb, xhi, xlo, shi, slo, part, r1, r2, across, along,
     sa_s, sa_r, sb_s, sb_r, sf_s, sf_r, s1_s, s1_r, s2_s, s2_r, sx_s, sy_s, so_r,
 ):
@@ -216,6 +210,7 @@
     own_b = jnp.where((z + zl // 4) % 2 == 0, 1, 0)
     own_o = jnp.where((panel == B) | (facing == B), 1, 0)
     out_count = jnp.where(gap == 0, 4, 8)
+    to_grid_order(j_ref, w_ref, first, second, y_ref, hi, lo, onehot, acc)
     pl.semaphore_wait(barrier, 3 + 15 + 8 + 7 + out_count - own_b - own_o)
 
     @pl.loop(0, 16)
@@ -317,11 +312,6 @@
         def _():
             send(part.at[q, upper], r2.at[k8, upper], s2_s.at[i, 0], s2_r.at[k8, 0], mate(i))
 
-    @pl.loop(0, 7)
-    def _(n):
-        i = turn(n, e)
-        send(part.at[8 * e + i, lower], r2.at[k8, lower], s2_s.at[i, 1], s2_r.at[k8, 1], mate(i))
-
     r2[k8] = part[8 * e + k8]
 
     for h, rows in enumerate((upper, lower)):
@@ -330,6 +320,13 @@
         def _(n):
             i = (k8 + 1 + n) % 8
             landed(r2.at[i, rows], s2_r.at[i, h])
+
+        if h == 0:
+
+            @pl.loop(0, 7)
+            def _(n):
+                i = turn(n, e)
+                send(part.at[8 * e + i, lower], r2.at[k8, lower], s2_s.at[i, 1], s2_r.at[k8, 1], mate(i))
 
         total = r2[0, rows]
         for i in range(1, 8):
@@ -370,7 +367,7 @@
             pl.loop(0, 2)(lambda i: sent(along.at[h, i], sy_s.at[h, i], (facing, 2 * h + i)))
 
 
-def band_part(spectral):
+def band_part(jacobian, cell_weight, first, second):
     lane = np.arange(128)
     x, layer = lane % 32, lane // 32
     near = np.abs(x[:, None] - x[None, :]) + np.abs(layer[:, None] - layer[None, :]) == 1
@@ -384,9 +381,14 @@
     return pl.pallas_call(
         band_kernel,
         out_shape=jax.ShapeDtypeStruct((7, 64, 256), F32),
-        in_specs=[vmem] * 3,
+        in_specs=[vmem] * 6,
         out_specs=vmem,
         scratch_shapes=[
+            pltpu.VMEM((16, 64, 256), F32),
+            pltpu.VMEM((512, 4096), BF16),
+            pltpu.VMEM((512, 4096), BF16),
+            pltpu.VMEM((512, 4096), BF16),
+            pltpu.VMEM((512, 512), F32),
             pltpu.VMEM((16, 64, 256), F32),
             pltpu.VMEM((28, 64, 256), F32),
             pltpu.VMEM((1536, 256), BF16),
@@ -400,13 +402,13 @@
             pltpu.VMEM((2, 2, 64, 256), F32),
         ]
         + [dma(c) for c in counts],
-        compiler_params=pltpu.CompilerParams(collective_id=0, has_side_effects=True, vmem_limit_bytes=40 * 2**20),
-    )(spectral, lam, adjacency)
+        compiler_params=pltpu.CompilerParams(collective_id=0, has_side_effects=True, vmem_limit_bytes=48 * 2**20),
+    )(jacobian, cell_weight.reshape(32, 128), first, second, lam, adjacency)
 
 
 def per_device(jacobian, cell_weight, neighbors):
-    spectral = local_part(jacobian, cell_weight, neighbors)
-    return jnp.swapaxes(band_part(spectral), 1, 2)
+    first, second = places(neighbors)
+    return jnp.swapaxes(band_part(jacobian, cell_weight, first, second), 1, 2)
 
 
 def solution(mesh):

time: 147 us -> 145 us (0.986)
  the two profiles are of different devices: /device:TPU:1 before, /device:TPU:455 now
where the time goes in v3:
time: 145 us
  Pallas kernels  140 us (97%)
  local copies, waits for them, and re-layouts  5.03 us (3%)
    pallas_call x1, Pallas kernels, band_part(): pl.pallas_call(band_kernel, out_shape=jax.ShapeDtypeStruct((7, 64, 256),...  136 us
    unnamed x14, local copies, waits for them, and re-layouts  5.03 us
    pallas_call x1, Pallas kernels, places(): pl.pallas_call(place_kernel, out_shape=[jax.ShapeDtypeStruct((32, 128), j...  3.98 us

profile of v3, /device:TPU:455, one launch (start us, length us, event | category | flops | bytes accessed | tf_op | source)
XLA Modules:
  0.0 145.1 jit_solution(15313747342421742015)
XLA Ops:
  0.0 0.0 copy-start.1
  0.0 1.6 %copy.8 = s32[1,6,32,128]{3,2,1,0:T(8,128)} copy(s32[1,6,32,128]{3,1,2,0:T(8,128)} %bitcast.9) | data formatting | bytes 196608
  1.6 0.0 copy-start.2
  1.6 0.0 copy-start.3
  1.6 4.0 %shard_map.55 = (s32[32,128]{1,0:T(8,128)}, s32[32,128]{1,0:T(8,128)}) custom-call(s32[6,32,128]{2,1,0:T(8,128)} %bitcast.8), custom_call_target="tpu_custom_call" | custom-call | tf_op jit(solution)/shard_map/pallas_call | solution.py:115
  5.6 0.0 copy-done.1
  5.6 0.0 copy-done.2
  5.6 0.0 copy-done.3
  5.6 0.0 copy-start
  5.6 1.2 copy-done
  6.8 0.0 copy-start.4
  6.8 0.7 copy-done.4
  7.5 0.0 copy-start.5
  7.5 0.7 copy-done.5
  8.3 136.1 %shard_map.56 = f32[7,64,256]{2,1,0:T(8,128)S(1)} custom-call(f32[64,4096]{1,0:T(8,128)S(1)} %copy-done, f32[32,128]{1,0:T(8,128)S(1)} %bitcast.7, s32[32,128]{1,0:T(8,128)S(1)} %copy-done.4, s32[32,128]{1,0:T(8,128)S(1)} %copy-done.5, f32[16,256]{1,0:T(8,128)S(1)} %copy-done.3, bf16[256,256]{1,0:T(8,128)(2,1)S(1)} %copy-done.1), custom_call_target="tpu_custom_call" | custom-call | tf_op jit(solution)/shard_map/pallas_call | solution.py:381
  144.4 0.8 copy.10
Async XLA Ops:
  0.0 5.6 %copy-start.1 = (bf16[256,256]{1,0:T(8,128)(2,1)S(1)}, bf16[256,256]{1,0:T(8,128)(2,1)}, u32[]{:S(2)}) copy-start(bf16[256,256]{1,0:T(8,128)(2,1)} %constant.4.clone.adj_ref) | copy-start | bytes 393220
  1.6 4.0 %copy-start.2 = (f32[4096]{0:T(1024)S(1)}, f32[4096]{0:T(1024)}, u32[]{:S(2)}) copy-start(f32[4096]{0:T(1024)} %param.6) | copy-start | bytes 49156
  1.6 4.0 %copy-start.3 = (f32[16,256]{1,0:T(8,128)S(1)}, f32[16,256]{1,0:T(8,128)}, u32[]{:S(2)}) copy-start(f32[16,256]{1,0:T(8,128)} %constant.5.clone.lam_ref) | copy-start | bytes 49156
  5.6 1.2 copy-start
  6.8 0.7 copy-start.4
  7.5 0.7 copy-start.5

commit v4 on v3

--- a/solution.py
+++ b/solution.py
@@ -41,7 +41,10 @@
     return value >> 12
 
 
-def place_kernel(nb_ref, first, second, table):
+def place_kernel(rows_ref, first, second, table, nb_ref):
+    for s in range(32):
+        for d in range(6):
+            nb_ref[d, s : s + 1, :] = rows_ref[d : d + 1, 128 * s : 128 * s + 128]
     own = lax.broadcasted_iota(jnp.int32, (32, 128), 0) * 128 + lax.broadcasted_iota(jnp.int32, (32, 128), 1)
     missing = [jnp.where(nb_ref[d] < 0, 1.0, 0.0).astype(F32) for d in range(6)]
     count = [jnp.sum(m) for m in missing]
@@ -117,8 +120,8 @@
         out_shape=[jax.ShapeDtypeStruct((32, 128), jnp.int32)] * 2,
         in_specs=[vmem],
         out_specs=[vmem] * 2,
-        scratch_shapes=[pltpu.VMEM((32, 128), jnp.int32)],
-    )(neighbors.reshape(6, 32, 128))
+        scratch_shapes=[pltpu.VMEM((32, 128), jnp.int32), pltpu.VMEM((6, 32, 128), jnp.int32)],
+    )(neighbors)
 
 
 def task_place(t, k8, e):
@@ -131,10 +134,10 @@
 
 
 def band_kernel(
-    j_ref, w_ref, first, second, lam_ref, adj_ref, o_ref,
-    y_ref, hi, lo, onehot, acc,
+    far_ref, w_ref, first, second, lam_ref, adj_ref, o_ref,
+    j_ref, y_ref, hi, lo, onehot, acc,
     ra, rb, xhi, xlo, shi, slo, part, r1, r2, across, along,
-    sa_s, sa_r, sb_s, sb_r, sf_s, sf_r, s1_s, s1_r, s2_s, s2_r, sx_s, sy_s, so_r,
+    sa_s, sa_r, sb_s, sb_r, sf_s, sf_r, s1_s, s1_r, s2_s, s2_r, sx_s, sy_s, so_r, j_sem,
 ):
     B, R = lax.axis_index("blk"), lax.axis_index("rep")
     pln, zl, zh, e = B // 8, B % 8, R // 2, R % 2
@@ -192,6 +195,8 @@
         j = jnp.where(m < 3, 3 - m, m - 3)
         return worked_on(jnp.where(m < 3, (B - j + 128) % 128, B), j)
 
+    fetched = pltpu.make_async_copy(far_ref, j_ref, j_sem.at[0])
+    fetched.start()
     barrier = pltpu.get_barrier_semaphore()
 
     def greet(place):
@@ -210,6 +215,7 @@
     own_b = jnp.where((z + zl // 4) % 2 == 0, 1, 0)
     own_o = jnp.where((panel == B) | (facing == B), 1, 0)
     out_count = jnp.where(gap == 0, 4, 8)
+    fetched.wait()
     to_grid_order(j_ref, w_ref, first, second, y_ref, hi, lo, onehot, acc)
     pl.semaphore_wait(barrier, 3 + 15 + 8 + 7 + out_count - own_b - own_o)
 
@@ -268,15 +274,6 @@
         x, top, rest = fetch(p)
         keep(p, top, rest)
         smoothed(p, x, top, rest)
-
-    @pl.loop(0, 2)
-    def _(p):
-        pl.loop(0, 4)(lambda s: landed(rb.at[16 + p * 4 + s], sf_r.at[p * 4 + s]))
-        x, top, rest = fetch(4 + p)
-        keep(4 + p, top, rest)
-
-    pl.loop(0, 4)(lambda s: landed(rb.at[24 + s], sf_r.at[8 + s]))
-    smoothed(4, *fetch(6))
 
     def tile(q):
         p, j = q // 4, q % 4
@@ -288,83 +285,77 @@
         total = total + lax.dot_general(slo[p, :], xhi[o, :], NT, preferred_element_type=F32)
         return total + lax.dot_general(shi[p, :], xhi[o, :], NT, preferred_element_type=F32)
 
-    def turn(n, core):
-        return jnp.where(n < 7, (k8 + 1 + (n + 3 * core + 2 * k8) % 7) % 8, k8)
-
-    @pl.loop(0, 8)
-    def _(n):
-        i = turn(n, 1 - e)
+    def inner(n, core):
+        m = (n + k8) % 3
+        return jnp.where(core == 0, (n + k8) % 7, m + 2 * (m // 2))
+
+    def outer(n, core):
+        m = (n + k8) % 5
+        return jnp.where(core == 0, 7, jnp.where(m < 2, m + 2, m + 3))
+
+    def for_other(i):
         q = 8 * (1 - e) + i
         part[q] = tile(q)
         send(part.at[q], r1.at[i], s1_s.at[i], s1_r.at[i], other)
 
-    upper, lower = pl.ds(0, 128), pl.ds(128, 128)
-
-    @pl.loop(0, 8)
-    def _(n):
-        i = turn(n, e)
+    def for_us(i):
         q = 8 * e + i
         total = tile(q)
         landed(r1.at[i], s1_r.at[i])
         part[q] = total + r1[i]
 
-        @pl.when(n < 7)
+        @pl.when(i != k8)
         def _():
-            send(part.at[q, upper], r2.at[k8, upper], s2_s.at[i, 0], s2_r.at[k8, 0], mate(i))
-
+            send(part.at[q], r2.at[k8], s2_s.at[i], s2_r.at[k8], mate(i))
+
+    pl.loop(0, 3 + 4 * e)(lambda n: for_other(inner(n, 1 - e)))
+    pl.loop(0, 7 - 4 * e)(lambda n: for_us(inner(n, e)))
+
+    @pl.loop(0, 2)
+    def _(p):
+        pl.loop(0, 4)(lambda s: landed(rb.at[16 + p * 4 + s], sf_r.at[p * 4 + s]))
+        x, top, rest = fetch(4 + p)
+        keep(4 + p, top, rest)
+
+    pl.loop(0, 4)(lambda s: landed(rb.at[24 + s], sf_r.at[8 + s]))
+    smoothed(4, *fetch(6))
+    pl.loop(0, 5 - 4 * e)(lambda n: for_other(outer(n, 1 - e)))
+    pl.loop(0, 1 + 4 * e)(lambda n: for_us(outer(n, e)))
     r2[k8] = part[8 * e + k8]
 
-    for h, rows in enumerate((upper, lower)):
-
-        @pl.loop(0, 7)
-        def _(n):
-            i = (k8 + 1 + n) % 8
-            landed(r2.at[i, rows], s2_r.at[i, h])
-
-        if h == 0:
-
-            @pl.loop(0, 7)
-            def _(n):
-                i = turn(n, e)
-                send(part.at[8 * e + i, lower], r2.at[k8, lower], s2_s.at[i, 1], s2_r.at[k8, 1], mate(i))
-
-        total = r2[0, rows]
-        for i in range(1, 8):
-            total = total + r2[i, rows]
-        across[h] = total.T.reshape(4, 64, 128)
-        along[h] = total.reshape(2, 64, 256)
-
-        @pl.loop(0, 4)
-        def _(i):
-            r = (i + pln) % 4
-            send(across.at[h, r], o_ref.at[3 + gap, :, rows], sx_s.at[h, r], so_r.at[3 + gap, h], (panel, r))
+    @pl.loop(0, 7)
+    def _(n):
+        i = (k8 + 1 + n) % 8
+        landed(r2.at[i], s2_r.at[i])
+
+    total = r2[0]
+    for i in range(1, 8):
+        total = total + r2[i]
+    along[...] = total.reshape(4, 64, 256)
+    across[...] = total.T.reshape(4, 64, 256)
+
+    @pl.loop(0, 4)
+    def _(i):
+        r = (i + pln) % 4
+        send(across.at[r], o_ref.at[3 + gap], sx_s.at[r], so_r.at[3 + gap], (panel, r))
 
         @pl.when(gap >= 1)
         def _():
-            @pl.loop(0, 2)
-            def _(i):
-                send(along.at[h, i], o_ref.at[3 - gap], sy_s.at[h, i], so_r.at[3 - gap, 0], (facing, 2 * h + i))
-
-    pl.loop(0, 3)(lambda m: landed(o_ref.at[m], so_r.at[m, 0]))
-
-    @pl.loop(3, 7)
-    def _(m):
-        landed(o_ref.at[m, :, upper], so_r.at[m, 0])
-        landed(o_ref.at[m, :, lower], so_r.at[m, 1])
+            send(along.at[r], o_ref.at[3 - gap], sy_s.at[r], so_r.at[3 - gap], (facing, r))
+
+    pl.loop(0, 7)(lambda m: landed(o_ref.at[m], so_r.at[m]))
 
     pl.loop(0, 16)(lambda k: sent(y_ref.at[k], sa_s.at[k], a_to(k)))
     pl.loop(0, 16)(lambda s: sent(ra.at[s], sb_s.at[s], b_to(s // 2)))
     pl.loop(0, 8)(lambda s: sent(rb.at[s], sf_s.at[s], down))
     pl.loop(0, 4)(lambda s: sent(rb.at[12 + s], sf_s.at[8 + s], up))
     pl.loop(0, 8)(lambda i: sent(part.at[8 * (1 - e) + i], s1_s.at[i], other))
-
-    for h, rows in enumerate((upper, lower)):
-        pl.loop(0, 8)(lambda i: sent(part.at[8 * e + i, rows], s2_s.at[i, h], mate(i)))
-        pl.loop(0, 4)(lambda r: sent(across.at[h, r], sx_s.at[h, r], (panel, r)))
-
-        @pl.when(gap >= 1)
-        def _():
-            pl.loop(0, 2)(lambda i: sent(along.at[h, i], sy_s.at[h, i], (facing, 2 * h + i)))
+    pl.loop(0, 8)(lambda i: sent(part.at[8 * e + i], s2_s.at[i], mate(i)))
+    pl.loop(0, 4)(lambda r: sent(across.at[r], sx_s.at[r], (panel, r)))
+
+    @pl.when(gap >= 1)
+    def _():
+        pl.loop(0, 4)(lambda r: sent(along.at[r], sy_s.at[r], (facing, r)))
 
 
 def band_part(jacobian, cell_weight, first, second):
@@ -377,13 +368,14 @@
     lam = jnp.asarray(np.repeat(lam, 128).reshape(16, 256), F32)
     vmem = pl.BlockSpec(memory_space=pltpu.VMEM)
     dma = pltpu.SemaphoreType.DMA
-    counts = ((16,),) * 4 + ((12,),) * 2 + ((8,),) * 2 + ((8, 2),) * 2 + ((2, 4), (2, 2), (7, 2))
+    counts = ((16,),) * 4 + ((12,),) * 2 + ((8,),) * 4 + ((4,), (4,), (7,), (1,))
     return pl.pallas_call(
         band_kernel,
         out_shape=jax.ShapeDtypeStruct((7, 64, 256), F32),
-        in_specs=[vmem] * 6,
+        in_specs=[pl.BlockSpec(memory_space=pl.ANY)] + [vmem] * 5,
         out_specs=vmem,
         scratch_shapes=[
+            pltpu.VMEM((64, 4096), F32),
             pltpu.VMEM((16, 64, 256), F32),
             pltpu.VMEM((512, 4096), BF16),
             pltpu.VMEM((512, 4096), BF16),
@@ -398,8 +390,8 @@
             pltpu.VMEM((16, 256, 256), F32),
             pltpu.VMEM((8, 256, 256), F32),
             pltpu.VMEM((8, 256, 256), F32),
-            pltpu.VMEM((2, 4, 64, 128), F32),
-            pltpu.VMEM((2, 2, 64, 256), F32),
+            pltpu.VMEM((4, 64, 256), F32),
+            pltpu.VMEM((4, 64, 256), F32),
         ]
         + [dma(c) for c in counts],
         compiler_params=pltpu.CompilerParams(collective_id=0, has_side_effects=True, vmem_limit_bytes=48 * 2**20),

time: 145 us -> 149 us (1.028)
  the two profiles are of different devices: /device:TPU:455 before, /device:TPU:1 now
where the time goes in v4:
time: 149 us; the launch traced here: 148 us
  Pallas kernels  143 us (96%)
  local copies, waits for them, and re-layouts  4.87 us (3%)
    pallas_call x1, Pallas kernels, band_part(): pl.pallas_call(band_kernel, out_shape=jax.ShapeDtypeStruct((7, 64, 256),...  139 us
    unnamed x13, local copies, waits for them, and re-layouts  4.87 us
    pallas_call x1, Pallas kernels, places(): pl.pallas_call(place_kernel, out_shape=[jax.ShapeDtypeStruct((32, 128), j...  4.1 us

profile of v4, /device:TPU:1, one launch (start us, length us, event | category | flops | bytes accessed | tf_op | source)
XLA Modules:
  0.0 148.1 jit_solution(3044485630209782028)
XLA Ops:
  0.0 0.0 copy-start.1
  0.0 4.1 %shard_map.55 = (s32[32,128]{1,0:T(8,128)}, s32[32,128]{1,0:T(8,128)}) custom-call(s32[6,4096]{1,0:T(8,128)} %rows_ref.1), custom_call_target="tpu_custom_call" | custom-call | tf_op jit(solution)/shard_map/pallas_call | solution.py:118
  4.1 0.0 copy-done.1
  4.1 0.0 copy-start
  4.1 1.2 copy-done
  5.3 0.0 copy-start.2
  5.3 0.7 copy-done.2
  6.0 0.0 copy-start.3
  6.1 0.7 copy-done.3
  6.8 0.0 copy-start.4
  6.8 0.7 copy-done.4
  7.5 0.0 copy-start.5
  7.5 0.7 copy-done.5
  8.2 139.2 %shard_map.56 = f32[7,64,256]{2,1,0:T(8,128)S(1)} custom-call(f32[64,4096]{1,0:T(8,128)S(1)} %copy-done, f32[32,128]{1,0:T(8,128)S(1)} %bitcast.3, s32[32,128]{1,0:T(8,128)S(1)} %copy-done.4, s32[32,128]{1,0:T(8,128)S(1)} %copy-done.5, f32[16,256]{1,0:T(8,128)S(1)} %copy-done.3, bf16[256,256]{1,0:T(8,128)(2,1)S(1)} %copy-done.1), custom_call_target="tpu_custom_call" | custom-call | tf_op jit(solution)/shard_map/pallas_call | solution.py:372
  147.4 0.8 copy.7
Async XLA Ops:
  0.0 4.1 %copy-start.1 = (bf16[256,256]{1,0:T(8,128)(2,1)S(1)}, bf16[256,256]{1,0:T(8,128)(2,1)}, u32[]{:S(2)}) copy-start(bf16[256,256]{1,0:T(8,128)(2,1)} %constant.4.clone.adj_ref) | copy-start | bytes 393220
  4.1 1.2 copy-start
  5.3 0.7 copy-start.2
  6.0 0.7 copy-start.3
  6.8 0.7 copy-start.4
  7.5 0.7 copy-start.5

commit v5 on v4

--- a/solution.py
+++ b/solution.py
@@ -221,12 +221,12 @@
 
     @pl.loop(0, 16)
     def _(n):
-        k = 2 * ((k8 + n // 2 + z + 4 * (n % 2)) % 8) + n % 2
+        k = 2 * ((k8 + 32 - z // 2 - n // 2 - 4 * (n % 2)) % 8) + n % 2
         send(y_ref.at[k], ra.at[2 * k8 + e], sa_s.at[k], sa_r.at[2 * k8 + e], a_to(k))
 
     @pl.loop(0, 16)
     def _(n):
-        i = (k8 + 32 - z - 4 * e - n // 2) % 8
+        i = (k8 + z // 2 + n // 2 + 4 * e) % 8
         s = 2 * i + n % 2
         landed(ra.at[s], sa_r.at[s])
         slot = (zl % 4) * 4 + zh * 2 + n % 2
@@ -336,7 +336,7 @@
 
     @pl.loop(0, 4)
     def _(i):
-        r = (i + pln) % 4
+        r = 2 * ((i + e + z) % 2) + (i // 2 + pln) % 2
         send(across.at[r], o_ref.at[3 + gap], sx_s.at[r], so_r.at[3 + gap], (panel, r))
 
         @pl.when(gap >= 1)

time: 149 us -> 149 us (level)
  the two profiles are of different devices: /device:TPU:1 before, /device:TPU:12 now
where the time goes in v5:
time: 149 us
  Pallas kernels  144 us (97%)
  local copies, waits for them, and re-layouts  4.87 us (3%)
    pallas_call x1, Pallas kernels, band_part(): pl.pallas_call(band_kernel, out_shape=jax.ShapeDtypeStruct((7, 64, 256),...  140 us
    unnamed x13, local copies, waits for them, and re-layouts  4.87 us
    pallas_call x1, Pallas kernels, places(): pl.pallas_call(place_kernel, out_shape=[jax.ShapeDtypeStruct((32, 128), j...  4.1 us

profile of v5, /device:TPU:12, one launch (start us, length us, event | category | flops | bytes accessed | tf_op | source)
XLA Modules:
  0.0 148.9 jit_solution(938736504227550843)
XLA Ops:
  0.0 0.0 copy-start.1
  0.0 4.1 %shard_map.55 = (s32[32,128]{1,0:T(8,128)}, s32[32,128]{1,0:T(8,128)}) custom-call(s32[6,4096]{1,0:T(8,128)} %rows_ref.1), custom_call_target="tpu_custom_call" | custom-call | tf_op jit(solution)/shard_map/pallas_call | solution.py:118
  4.1 0.0 copy-done.1
  4.1 0.0 copy-start
  4.1 1.2 copy-done
  5.3 0.0 copy-start.2
  5.3 0.7 copy-done.2
  6.0 0.0 copy-start.3
  6.1 0.7 copy-done.3
  6.8 0.0 copy-start.4
  6.8 0.7 copy-done.4
  7.5 0.0 copy-start.5
  7.5 0.7 copy-done.5
  8.2 140.0 %shard_map.56 = f32[7,64,256]{2,1,0:T(8,128)S(1)} custom-call(f32[64,4096]{1,0:T(8,128)S(1)} %copy-done, f32[32,128]{1,0:T(8,128)S(1)} %bitcast.3, s32[32,128]{1,0:T(8,128)S(1)} %copy-done.4, s32[32,128]{1,0:T(8,128)S(1)} %copy-done.5, f32[16,256]{1,0:T(8,128)S(1)} %copy-done.3, bf16[256,256]{1,0:T(8,128)(2,1)S(1)} %copy-done.1), custom_call_target="tpu_custom_call" | custom-call | tf_op jit(solution)/shard_map/pallas_call | solution.py:372
  148.2 0.8 copy.7
Async XLA Ops:
  0.0 4.1 %copy-start.1 = (bf16[256,256]{1,0:T(8,128)(2,1)S(1)}, bf16[256,256]{1,0:T(8,128)(2,1)}, u32[]{:S(2)}) copy-start(bf16[256,256]{1,0:T(8,128)(2,1)} %constant.4.clone.adj_ref) | copy-start | bytes 393220
  4.1 1.2 copy-start
  5.3 0.7 copy-start.2
  6.0 0.7 copy-start.3
  6.8 0.7 copy-start.4
  7.5 0.7 copy-start.5

commit v6 on v4

--- a/solution.py
+++ b/solution.py
@@ -286,11 +286,11 @@
         return total + lax.dot_general(shi[p, :], xhi[o, :], NT, preferred_element_type=F32)
 
     def inner(n, core):
-        m = (n + k8) % 3
-        return jnp.where(core == 0, (n + k8) % 7, m + 2 * (m // 2))
+        m = (n + 2 * k8) % 3
+        return jnp.where(core == 0, (n + 3 * k8) % 7, m + 2 * (m // 2))
 
     def outer(n, core):
-        m = (n + k8) % 5
+        m = (n + 3 * k8) % 5
         return jnp.where(core == 0, 7, jnp.where(m < 2, m + 2, m + 3))
 
     def for_other(i):
@@ -336,7 +336,7 @@
 
     @pl.loop(0, 4)
     def _(i):
-        r = (i + pln) % 4
+        r = 2 * ((i + e + z) % 2) + (i // 2 + pln) % 2
         send(across.at[r], o_ref.at[3 + gap], sx_s.at[r], so_r.at[3 + gap], (panel, r))
 
         @pl.when(gap >= 1)

time: 149 us -> 150 us (level)
  the two profiles are of different devices: /device:TPU:1 before, /device:TPU:28 now
where the time goes in v6:
time: 150 us; the launch traced here: 149 us
  Pallas kernels  144 us (96%)
  local copies, waits for them, and re-layouts  4.87 us (3%)
    pallas_call x1, Pallas kernels, band_part(): pl.pallas_call(band_kernel, out_shape=jax.ShapeDtypeStruct((7, 64, 256),...  140 us
    unnamed x13, local copies, waits for them, and re-layouts  4.87 us
    pallas_call x1, Pallas kernels, places(): pl.pallas_call(place_kernel, out_shape=[jax.ShapeDtypeStruct((32, 128), j...  4.1 us

profile of v6, /device:TPU:28, one launch (start us, length us, event | category | flops | bytes accessed | tf_op | source)
XLA Modules:
  0.0 149.2 jit_solution(8394713498881847059)
XLA Ops:
  0.0 0.0 copy-start.1
  0.0 4.1 %shard_map.55 = (s32[32,128]{1,0:T(8,128)}, s32[32,128]{1,0:T(8,128)}) custom-call(s32[6,4096]{1,0:T(8,128)} %rows_ref.1), custom_call_target="tpu_custom_call" | custom-call | tf_op jit(solution)/shard_map/pallas_call | solution.py:118
  4.1 0.0 copy-done.1
  4.1 0.0 copy-start
  4.1 1.2 copy-done
  5.3 0.0 copy-start.2
  5.3 0.7 copy-done.2
  6.0 0.0 copy-start.3
  6.1 0.7 copy-done.3
  6.8 0.0 copy-start.4
  6.8 0.7 copy-done.4
  7.5 0.0 copy-start.5
  7.5 0.7 copy-done.5
  8.2 140.2 %shard_map.56 = f32[7,64,256]{2,1,0:T(8,128)S(1)} custom-call(f32[64,4096]{1,0:T(8,128)S(1)} %copy-done, f32[32,128]{1,0:T(8,128)S(1)} %bitcast.3, s32[32,128]{1,0:T(8,128)S(1)} %copy-done.4, s32[32,128]{1,0:T(8,128)S(1)} %copy-done.5, f32[16,256]{1,0:T(8,128)S(1)} %copy-done.3, bf16[256,256]{1,0:T(8,128)(2,1)S(1)} %copy-done.1), custom_call_target="tpu_custom_call" | custom-call | tf_op jit(solution)/shard_map/pallas_call | solution.py:372
  148.5 0.8 copy.7
Async XLA Ops:
  0.0 4.1 %copy-start.1 = (bf16[256,256]{1,0:T(8,128)(2,1)S(1)}, bf16[256,256]{1,0:T(8,128)(2,1)}, u32[]{:S(2)}) copy-start(bf16[256,256]{1,0:T(8,128)(2,1)} %constant.4.clone.adj_ref) | copy-start | bytes 393220
  4.1 1.2 copy-start
  5.3 0.7 copy-start.2
  6.0 0.7 copy-start.3
  6.8 0.7 copy-start.4
  7.5 0.7 copy-start.5

commit v7 on v3

--- a/solution.py
+++ b/solution.py
@@ -41,7 +41,10 @@
     return value >> 12
 
 
-def place_kernel(nb_ref, first, second, table):
+def place_kernel(rows_ref, first, second, table, nb_ref):
+    for s in range(32):
+        for d in range(6):
+            nb_ref[d, s : s + 1, :] = rows_ref[d : d + 1, 128 * s : 128 * s + 128]
     own = lax.broadcasted_iota(jnp.int32, (32, 128), 0) * 128 + lax.broadcasted_iota(jnp.int32, (32, 128), 1)
     missing = [jnp.where(nb_ref[d] < 0, 1.0, 0.0).astype(F32) for d in range(6)]
     count = [jnp.sum(m) for m in missing]
@@ -117,8 +120,8 @@
         out_shape=[jax.ShapeDtypeStruct((32, 128), jnp.int32)] * 2,
         in_specs=[vmem],
         out_specs=[vmem] * 2,
-        scratch_shapes=[pltpu.VMEM((32, 128), jnp.int32)],
-    )(neighbors.reshape(6, 32, 128))
+        scratch_shapes=[pltpu.VMEM((32, 128), jnp.int32), pltpu.VMEM((6, 32, 128), jnp.int32)],
+    )(neighbors)
 
 
 def task_place(t, k8, e):
@@ -131,10 +134,10 @@
 
 
 def band_kernel(
-    j_ref, w_ref, first, second, lam_ref, adj_ref, o_ref,
-    y_ref, hi, lo, onehot, acc,
+    far_j, far_w, far_first, far_second, far_lam, far_adj, o_ref,
+    j_ref, w_ref, first, second, lam_ref, adj_ref, y_ref, hi, lo, onehot, acc,
     ra, rb, xhi, xlo, shi, slo, part, r1, r2, across, along,
-    sa_s, sa_r, sb_s, sb_r, sf_s, sf_r, s1_s, s1_r, s2_s, s2_r, sx_s, sy_s, so_r,
+    sa_s, sa_r, sb_s, sb_r, sf_s, sf_r, s1_s, s1_r, s2_s, s2_r, sx_s, sy_s, so_r, in_sem,
 ):
     B, R = lax.axis_index("blk"), lax.axis_index("rep")
     pln, zl, zh, e = B // 8, B % 8, R // 2, R % 2
@@ -192,6 +195,17 @@
         j = jnp.where(m < 3, 3 - m, m - 3)
         return worked_on(jnp.where(m < 3, (B - j + 128) % 128, B), j)
 
+    fetched = [
+        pltpu.make_async_copy(far, near, in_sem.at[i])
+        for i, (far, near) in enumerate(
+            (
+                (far_j, j_ref), (far_w, w_ref), (far_first, first),
+                (far_second, second), (far_lam, lam_ref), (far_adj, adj_ref),
+            )
+        )
+    ]
+    for copy in fetched:
+        copy.start()
     barrier = pltpu.get_barrier_semaphore()
 
     def greet(place):
@@ -210,6 +224,8 @@
     own_b = jnp.where((z + zl // 4) % 2 == 0, 1, 0)
     own_o = jnp.where((panel == B) | (facing == B), 1, 0)
     out_count = jnp.where(gap == 0, 4, 8)
+    for copy in fetched:
+        copy.wait()
     to_grid_order(j_ref, w_ref, first, second, y_ref, hi, lo, onehot, acc)
     pl.semaphore_wait(barrier, 3 + 15 + 8 + 7 + out_count - own_b - own_o)
 
@@ -377,13 +393,19 @@
     lam = jnp.asarray(np.repeat(lam, 128).reshape(16, 256), F32)
     vmem = pl.BlockSpec(memory_space=pltpu.VMEM)
     dma = pltpu.SemaphoreType.DMA
-    counts = ((16,),) * 4 + ((12,),) * 2 + ((8,),) * 2 + ((8, 2),) * 2 + ((2, 4), (2, 2), (7, 2))
+    counts = ((16,),) * 4 + ((12,),) * 2 + ((8,),) * 2 + ((8, 2),) * 2 + ((2, 4), (2, 2), (7, 2), (6,))
     return pl.pallas_call(
         band_kernel,
         out_shape=jax.ShapeDtypeStruct((7, 64, 256), F32),
-        in_specs=[vmem] * 6,
+        in_specs=[pl.BlockSpec(memory_space=pl.ANY)] * 6,
         out_specs=vmem,
         scratch_shapes=[
+            pltpu.VMEM((64, 4096), F32),
+            pltpu.VMEM((32, 128), F32),
+            pltpu.VMEM((32, 128), jnp.int32),
+            pltpu.VMEM((32, 128), jnp.int32),
+            pltpu.VMEM((16, 256), F32),
+            pltpu.VMEM((256, 256), BF16),
             pltpu.VMEM((16, 64, 256), F32),
             pltpu.VMEM((512, 4096), BF16),
             pltpu.VMEM((512, 4096), BF16),

time: 145 us -> 147 us (1.014)
    unnamed x14 -> x13, local copies, waits for them, and re-layouts: 5.03 us -> 4.87 us
where the time goes in v7:
time: 147 us; the launch traced here: 146 us
  Pallas kernels  141 us (96%)
  local copies, waits for them, and re-layouts  4.87 us (3%)
    pallas_call x1, Pallas kernels, band_part(): pl.pallas_call(band_kernel, out_shape=jax.ShapeDtypeStruct((7, 64, 256),...  137 us
    unnamed x13, local copies, waits for them, and re-layouts  4.87 us
    pallas_call x1, Pallas kernels, places(): pl.pallas_call(place_kernel, out_shape=[jax.ShapeDtypeStruct((32, 128), j...  4.1 us

profile of v7, /device:TPU:455, one launch (start us, length us, event | category | flops | bytes accessed | tf_op | source)
XLA Modules:
  0.0 146.1 jit_solution(17268374210649343722)
XLA Ops:
  0.0 0.0 copy-start.1
  0.0 4.1 %shard_map.55 = (s32[32,128]{1,0:T(8,128)}, s32[32,128]{1,0:T(8,128)}) custom-call(s32[6,4096]{1,0:T(8,128)} %rows_ref.1), custom_call_target="tpu_custom_call" | custom-call | tf_op jit(solution)/shard_map/pallas_call | solution.py:118
  4.1 0.0 copy-done.1
  4.1 0.0 copy-start
  4.1 1.2 copy-done
  5.3 0.0 copy-start.2
  5.3 0.7 copy-done.2
  6.0 0.0 copy-start.3
  6.1 0.7 copy-done.3
  6.8 0.0 copy-start.4
  6.8 0.7 copy-done.4
  7.5 0.0 copy-start.5
  7.5 0.7 copy-done.5
  8.2 137.1 %shard_map.56 = f32[7,64,256]{2,1,0:T(8,128)S(1)} custom-call(f32[64,4096]{1,0:T(8,128)S(1)} %copy-done, f32[32,128]{1,0:T(8,128)S(1)} %bitcast.3, s32[32,128]{1,0:T(8,128)S(1)} %copy-done.4, s32[32,128]{1,0:T(8,128)S(1)} %copy-done.5, f32[16,256]{1,0:T(8,128)S(1)} %copy-done.3, bf16[256,256]{1,0:T(8,128)(2,1)S(1)} %copy-done.1), custom_call_target="tpu_custom_call" | custom-call | tf_op jit(solution)/shard_map/pallas_call | solution.py:397
  145.3 0.8 copy.7
Async XLA Ops:
  0.0 4.1 %copy-start.1 = (bf16[256,256]{1,0:T(8,128)(2,1)S(1)}, bf16[256,256]{1,0:T(8,128)(2,1)}, u32[]{:S(2)}) copy-start(bf16[256,256]{1,0:T(8,128)(2,1)} %constant.4.clone.far_adj) | copy-start | bytes 393220
  4.1 1.2 copy-start
  5.3 0.7 copy-start.2
  6.0 0.7 copy-start.3
  6.8 0.7 copy-start.4
  7.5 0.7 copy-start.5
